TPU v7x, 32 devices: a whole 2x2x4 slice. The times are simulated.
32 devices in a mesh: dp: 8 (over z, y), mp: 4 (over x, core).
Axes of the slice: x: 2, y: 2, z: 4, core: 2. Of those that a mesh axis runs over, the one named last changes fastest.
Arguments:
- char_ids: int32 [8192, 50], P('dp'), may hold values from 0 to 261
- embedding: bfloat16 [262, 16], replicated, may hold values from -6 to 6
- conv_weight: bfloat16 [7, 16, 2048], P(None, None, 'mp'), may hold values from -0.75 to 0.75
- conv_bias: bfloat16 [2048], P('mp'), may hold values from -3 to -1
- highway_weight: bfloat16 [2, 2048, 2, 2048], P(None, None, None, 'mp'), may hold values from -0.125 to 0.125
- highway_bias: bfloat16 [2, 2, 2048], P(None, None, 'mp'), may hold values from -3 to 3
- proj_weight: bfloat16 [2048, 512], P(None, 'mp'), may hold values from -0.125 to 0.125
- proj_bias: bfloat16 [512], P('mp'), may hold values from -3 to 3
- cotangent: bfloat16 [8192, 512], P('dp', 'mp'), may hold values from -6 to 6
Outputs:
- token_vectors: bfloat16 [8192, 512], P('dp', 'mp')
- embedding_grad: float32 [262, 16], replicated
- conv_weight_grad: float32 [7, 16, 2048], P(None, None, 'mp')
- conv_bias_grad: float32 [2048], P('mp')
- highway_weight_grad: float32 [2, 2048, 2, 2048], P(None, None, None, 'mp')
- highway_bias_grad: float32 [2, 2, 2048], P(None, None, 'mp')
- proj_weight_grad: float32 [2048, 512], P(None, 'mp')
- proj_bias_grad: float32 [512], P('mp')
All inputs are finite; a program needn't handle non-finite values.
Results may differ from a plain program's by a relative error of at most 0.014.
The roundings to bfloat16 on the way count: a program that leaves them out, or rounds other values in their place, can miss the bound.
Values may be sent and summed in bfloat16 or wider, within the bound.
No kernel may reach another device: no remote copies, remote signals or barrier semaphores. Data moves between devices by JAX's collectives and lax.ppermute only.
A program may use at most 192 MiB of HBM per device.

v0:
```python
import jax
import jax.numpy as jnp
from jax import lax
from jax.sharding import PartitionSpec as P

neg_large = -1e30


def bank_widths(first_col, amount, full_width):
    col_index = first_col + jnp.arange(amount, dtype=jnp.int32)
    widths = jnp.ones((amount,), jnp.int32)
    for divisor in (64, 32, 16, 8, 4, 2):
        widths = widths + (col_index >= full_width // divisor).astype(jnp.int32)
    return widths


def pick_block(row_count, ceiling):
    chosen = 1
    for candidate in range(1, min(row_count, ceiling) + 1):
        if row_count % candidate == 0:
            chosen = candidate
    return chosen


def conv_preact(block_ids, embedding, flat_w):
    onehot = (
        block_ids[:, :, None] == jnp.arange(embedding.shape[0], dtype=jnp.int32)[None, None, :]
    ).astype(jnp.bfloat16)
    char_vecs = jnp.einsum(
        "tpv,vc->tpc", onehot, embedding, preferred_element_type=jnp.float32
    ).astype(jnp.bfloat16)
    tap_count = flat_w.shape[0] // char_vecs.shape[2]
    char_count = char_vecs.shape[1]
    padded = jnp.pad(char_vecs, ((0, 0), (0, tap_count - 1), (0, 0)))
    unfolded = jnp.concatenate(
        [padded[:, offset : offset + char_count, :] for offset in range(tap_count)], axis=2
    )
    preact = jnp.einsum("tpk,kf->tpf", unfolded, flat_w, preferred_element_type=jnp.float32)
    return (preact, unfolded, onehot)


def pool_weights(preact, places_ok):
    peak_val = jnp.max(jnp.where(places_ok[None], preact, neg_large), axis=1)
    expo_terms = jnp.exp(jnp.where(places_ok[None], preact - peak_val[:, None, :], neg_large))
    denom_sum = jnp.sum(expo_terms, axis=1)
    return (peak_val + jnp.log(denom_sum), expo_terms / denom_sum[:, None, :])


def conv_forward(local_ids, embedding, flat_w, bias_f, places_ok):
    block_size = pick_block(local_ids.shape[0], 256)
    id_blocks = local_ids.reshape(-1, block_size, local_ids.shape[1])

    def one_block(block_ids):
        preact, _, _ = conv_preact(block_ids, embedding, flat_w)
        pooled, _ = pool_weights(preact, places_ok)
        return jax.nn.silu(pooled + bias_f).astype(jnp.bfloat16)

    return lax.map(one_block, id_blocks).reshape(local_ids.shape[0], flat_w.shape[1])


def conv_backward(local_ids, pooled_grad, embedding, flat_w, bias_f, places_ok):
    block_size = pick_block(local_ids.shape[0], 256)
    id_blocks = local_ids.reshape(-1, block_size, local_ids.shape[1])
    grad_blocks = pooled_grad.reshape(-1, block_size, flat_w.shape[1])
    char_dim = embedding.shape[1]
    tap_count = flat_w.shape[0] // char_dim

    def one_block(carry, paired):
        block_ids, block_grad = paired
        preact, unfolded, onehot = conv_preact(block_ids, embedding, flat_w)
        pooled, weights = pool_weights(preact, places_ok)
        shifted = pooled + bias_f
        sig_vals = jax.nn.sigmoid(shifted)
        pool_grad = block_grad.astype(jnp.float32) * sig_vals * (1.0 + shifted * (1.0 - sig_vals))
        pre_grad = (weights * pool_grad[:, None, :]).astype(jnp.bfloat16)
        weight_acc = carry[0] + jnp.einsum(
            "tpk,tpf->kf", unfolded, pre_grad, preferred_element_type=jnp.float32
        )
        bias_acc = carry[1] + jnp.sum(pool_grad, axis=0)
        unf_grad = jnp.einsum("tpf,kf->tpk", pre_grad, flat_w, preferred_element_type=jnp.float32)
        char_count = unf_grad.shape[1]
        pieces = unf_grad.reshape(unf_grad.shape[0], char_count, tap_count, char_dim)
        char_grad = jnp.zeros(
            (unf_grad.shape[0], char_count + tap_count - 1, char_dim), jnp.float32
        )
        for offset in range(tap_count):
            char_grad = char_grad.at[:, offset : offset + char_count, :].add(
                pieces[:, :, offset, :]
            )
        char_grad = char_grad[:, :char_count, :]
        embed_acc = carry[2] + jnp.einsum(
            "tpv,tpc->vc", onehot.astype(jnp.float32), char_grad, precision=lax.Precision.HIGHEST
        )
        return ((weight_acc, bias_acc, embed_acc), None)

    start_vals = (
        jnp.zeros(flat_w.shape, jnp.float32),
        jnp.zeros((flat_w.shape[1],), jnp.float32),
        jnp.zeros(embedding.shape, jnp.float32),
    )
    totals, _ = lax.scan(one_block, start_vals, (id_blocks, grad_blocks))
    return totals


def sum_features(partial_value):
    return lax.psum_scatter(partial_value, "mp", scatter_dimension=1, tiled=True)


def on_device(
    char_ids,
    embedding,
    conv_weight,
    conv_bias,
    highway_weight,
    highway_bias,
    proj_weight,
    proj_bias,
    cotangent,
):
    mp_rank = lax.axis_index("mp")
    levels = highway_weight.shape[0]
    full_width = highway_weight.shape[1]
    columns = highway_weight.shape[3]
    tap_count = conv_weight.shape[0]
    char_dim = conv_weight.shape[1]
    char_count = char_ids.shape[1]
    first_col = mp_rank * conv_weight.shape[2]
    bank_width = conv_weight.shape[2]
    widths = bank_widths(first_col, bank_width, full_width)
    tap_ok = jnp.arange(tap_count)[:, None] < widths[None, :]
    places_ok = jnp.arange(char_count)[:, None] <= char_count - widths[None, :]
    flat_w = (conv_weight * tap_ok[:, None, :].astype(jnp.bfloat16)).reshape(
        tap_count * char_dim, bank_width
    )
    bias_f = conv_bias.astype(jnp.float32)
    pooled_out = conv_forward(char_ids, embedding, flat_w, bias_f, places_ok)
    layer_in = lax.all_gather(pooled_out, "mp", axis=1, tiled=True)
    own_start = mp_rank * columns
    kept_in = []
    kept_mix = []
    for number in range(levels):
        level_w = highway_weight[number].reshape(full_width, 2 * columns)
        mixed_in = jnp.dot(layer_in, level_w, preferred_element_type=jnp.float32)
        mixed_in = mixed_in + highway_bias[number].reshape(2 * columns).astype(jnp.float32)
        gating = jax.nn.sigmoid(mixed_in[:, columns:])
        own_cols = lax.dynamic_slice_in_dim(layer_in, own_start, columns, 1).astype(jnp.float32)
        update = gating * own_cols + (1.0 - gating) * jax.nn.silu(mixed_in[:, :columns])
        kept_in.append(layer_in)
        kept_mix.append(mixed_in)
        layer_in = lax.all_gather(update.astype(jnp.bfloat16), "mp", axis=1, tiled=True)
    token_vectors = (
        jnp.dot(layer_in, proj_weight, preferred_element_type=jnp.float32)
        + proj_bias.astype(jnp.float32)
    ).astype(jnp.bfloat16)
    proj_w_grad = jnp.einsum("tf,te->fe", layer_in, cotangent, preferred_element_type=jnp.float32)
    proj_b_grad = jnp.sum(cotangent.astype(jnp.float32), axis=0)
    partial_value = jnp.einsum(
        "te,fe->tf", cotangent, proj_weight, preferred_element_type=jnp.float32
    )
    level_grad = sum_features(partial_value).astype(jnp.bfloat16)
    w_grads = [None] * levels
    b_grads = [None] * levels
    pooled_grad = level_grad
    for number in range(levels - 1, -1, -1):
        mixed_in = kept_mix[number]
        level_in = kept_in[number]
        trans_in = mixed_in[:, :columns]
        gating = jax.nn.sigmoid(mixed_in[:, columns:])
        trans_sig = jax.nn.sigmoid(trans_in)
        smooth = trans_in * trans_sig
        own_cols = lax.dynamic_slice_in_dim(level_in, own_start, columns, 1).astype(jnp.float32)
        upstream = level_grad.astype(jnp.float32)
        gate_grad = upstream * (own_cols - smooth) * gating * (1.0 - gating)
        trans_grad = upstream * (1.0 - gating) * trans_sig * (1.0 + trans_in * (1.0 - trans_sig))
        mix_grad = jnp.concatenate([trans_grad, gate_grad], axis=1).astype(jnp.bfloat16)
        w_grad = jnp.einsum(
            "tf,tc->fc", level_in, mix_grad, preferred_element_type=jnp.float32
        ).reshape(full_width, 2, columns)
        b_grad = jnp.sum(mix_grad.astype(jnp.float32), axis=0).reshape(2, columns)
        w_grads[number] = w_grad
        b_grads[number] = b_grad
        level_w = highway_weight[number].reshape(full_width, 2 * columns)
        partial_value = jnp.einsum(
            "tc,fc->tf", mix_grad, level_w, preferred_element_type=jnp.float32
        )
        own_part = (
            lax.dynamic_slice_in_dim(partial_value, own_start, columns, 1) + gating * upstream
        )
        partial_value = lax.dynamic_update_slice_in_dim(partial_value, own_part, own_start, 1)
        if number > 0:
            level_grad = sum_features(partial_value).astype(jnp.bfloat16)
        else:
            pooled_grad = lax.psum_scatter(
                partial_value, "mp", scatter_dimension=1, tiled=True
            ).astype(jnp.bfloat16)
    high_w_grad = jnp.stack(w_grads, axis=0)
    high_b_grad = jnp.stack(b_grads, axis=0)
    weight_acc, bias_acc, embed_acc = conv_backward(
        char_ids, pooled_grad, embedding, flat_w, bias_f, places_ok
    )
    conv_w_grad = weight_acc.reshape(tap_count, char_dim, bank_width) * tap_ok[:, None, :].astype(
        jnp.float32
    )
    conv_b_grad = bias_acc
    embed_grad = lax.psum(embed_acc, ("dp", "mp"))
    conv_w_grad, conv_b_grad, high_w_grad, high_b_grad, proj_w_grad, proj_b_grad = lax.psum(
        (conv_w_grad, conv_b_grad, high_w_grad, high_b_grad, proj_w_grad, proj_b_grad), "dp"
    )
    return (
        token_vectors,
        embed_grad,
        conv_w_grad,
        conv_b_grad,
        high_w_grad,
        high_b_grad,
        proj_w_grad,
        proj_b_grad,
    )


def solution(mesh):
    in_specs = (
        P("dp", None),
        P(),
        P(None, None, "mp"),
        P("mp"),
        P(None, None, None, "mp"),
        P(None, None, "mp"),
        P(None, "mp"),
        P("mp"),
        P("dp", "mp"),
    )
    out_specs = (
        P("dp", "mp"),
        P(),
        P(None, None, "mp"),
        P("mp"),
        P(None, None, None, "mp"),
        P(None, None, "mp"),
        P(None, "mp"),
        P("mp"),
    )
    return jax.shard_map(
        on_device, mesh=mesh, in_specs=in_specs, out_specs=out_specs, check_vma=False
    )
```

profile of v0, /device:TPU:0, one launch (start us, length us, event | category | flops | bytes accessed | tf_op | source)
XLA Modules:
  0.0 1292.1 jit_solution(7358071573931325800)
XLA Ops:
  10.6 100.3 %while.38 = (s32[]{:T(128)}, bf16[4,256,512]{2,1,0:T(8,128)(2,1)S(1)}, s32[4,256,50]{1,2,0:T(8,128)S(1)}, bf16[262,16]{0,1:T(8,128)(2,1)}, bf16[112,512]{1,0:T(8...) while((s32[]{:T(128)}, bf16[4,256,512]{2,1,0:T(8,128)(2,1)S(1)}, ...), condition=%wide.region_3.4_spmd.clone, body=%wide.region_0.3_spmd.clone.sunk | while | flops 1612328960 | bytes 64271644 | solution.py:58
  24.4 11.0 exponential_reduce_fusion.2
  49.4 11.0 exponential_reduce_fusion.2
  74.5 11.0 exponential_reduce_fusion.2
  99.6 11.0 exponential_reduce_fusion.2
  123.5 26.0 %all-gather.4.cloned.1.call-done = bf16[1024,2048]{0,1:T(8,128)(2,1)} async-done(((bf16[1024,512]{0,1:T(8,128)(2,1)}), bf16[1024,2048]{0,1:T(8,128)(2,1)}) %all-gather.4.cloned.1.call-update) | async-done | bytes 4194320 | tf_op jit(solution)/shard_map/all_gather | solution.py:137
  173.5 23.8 %all-gather.6.cloned.1.call-done = bf16[1024,2048]{0,1:T(8,128)(2,1)} async-done(((bf16[1024,512]{0,1:T(8,128)(2,1)}), bf16[1024,2048]{0,1:T(8,128)(2,1)}) %all-gather.6.cloned.1.call-update) | async-done | bytes 4194320 | tf_op jit(solution)/shard_map/all_gather | solution.py:150
  207.2 64.9 %reduce-scatter.4.cloned.1.call-done = f32[1024,512]{0,1:T(8,128)} async-done(((f32[1024,2048]{0,1:T(8,128)}), f32[1024,512]{0,1:T(8,128)}) %reduce-scatter.4.cloned.1.call-update) | async-done | bytes 2097168 | tf_op jit(solution)/shard_map/reduce_scatter | solution.py:106
  288.4 10.9 reduce-scatter.8.cloned.1.call-start
  299.3 60.4 %reduce-scatter.6.cloned.1.call-done = f32[1024,512]{0,1:T(8,128)} async-done(((f32[1024,2048]{0,1:T(8,128)}), f32[1024,512]{0,1:T(8,128)}) %reduce-scatter.6.cloned.1.call-update) | async-done | bytes 2097168 | tf_op jit(solution)/shard_map/reduce_scatter | solution.py:106
  388.1 10.8 fusion.69
  398.9 13.8 %copy.48 = f32[1,2048,2,512]{3,2,1,0:T(2,128)} copy(f32[1,2048,2,512]{1,3,2,0:T(8,128)} %bitcast.192) | data formatting | bytes 16777216 | tf_op jit(solution)/shard_map/stack;reshape | solution.py:196
  425.2 13.4 %copy.47 = f32[1,2048,2,512]{3,2,1,0:T(2,128)} copy(f32[1,2048,2,512]{1,3,2,0:T(8,128)} %bitcast.193) | data formatting | bytes 16777216 | tf_op jit(solution)/shard_map/stack;reshape | solution.py:196
  438.6 12.3 pad_maximum_fusion
  450.9 19.5 %reduce-scatter.8.cloned.1.call-done = f32[1024,512]{1,0:T(8,128)} async-done(((f32[1024,2048]{1,0:T(8,128)}), f32[1024,512]{1,0:T(8,128)}) %reduce-scatter.8.cloned.1.call-update) | async-done | bytes 2097168 | tf_op jit(solution)/shard_map/reduce_scatter | solution.py:193
  472.1 247.6 %while.39 = (s32[]{:T(128)}, f32[112,512]{1,0:T(8,128)S(1)}, f32[512]{0:T(512)S(1)}, f32[262,16]{0,1:T(8,128)S(1)}, s32[4,256,50]{1,2,0:T(8,128)S(1)}, /*index=5...) while((s32[]{:T(128)}, f32[112,512]{1,0:T(8,128)S(1)}, ...), condition=%wide.region_11.12_spmd.clone, body=%wide.region_7.11_spmd.clone.sunk | while | flops 5230362112 | bytes 287963968 | solution.py:101
  486.0 11.2 fusion.134
  547.8 11.2 fusion.134
  609.6 11.2 fusion.134
  671.4 11.2 fusion.134
  727.2 39.0 %all-reduce.3 = (f32[512]{0:T(512)}, f32[2,2,512]{2,1,0:T(2,128)}, f32[128]{0:T(128)}) all-reduce(f32[512]{0:T(512)S(1)} %get-tuple-element.365, f32[2,2,512]{2,1,0:T(2,128)S(1)} %pad_maximum_fusion.7, f32[128]{0:T(128)S(1)} %convert_reduce_fusion.2), channel_id=1, replica_groups=mesh['dp'=8,'mp'=4] {'dp'}, use_global_device_ids=true, to_apply=%region_14.15 | all-reduce | flops 2688 | bytes 21504 | tf_op jit(solution)/shard_map/psum | solution.py:206
  766.2 42.1 %psum.49 = f32[262,16]{0,1:T(8,128)} all-reduce(f32[262,16]{0,1:T(8,128)S(1)} %get-tuple-element.363), channel_id=1, replica_groups=mesh['dp'=8,'mp'=4] {'dp','mp'}, use_global_device_ids=true, to_apply=%region_12.13 | all-reduce | flops 4192 | bytes 33536 | tf_op jit(solution)/shard_map/psum | solution.py:205
  808.2 461.9 %all-reduce.7.cloned.1.call-done = (f32[7,16,512]{2,1,0:T(8,128)}, f32[2,2048,2,512]{3,2,1,0:T(2,128)}, f32[2048,128]{1,0:T(8,128)}) async-done(((f32[7,16,512]{2,1,0:T(8,128)}, f32[2,2048,2,512]{3,2,1,0:T(2,128)}, f32[2048,128]{1,0:T(8,128)}), (f32[7,16,512]{2,1,0:T(8,128)}, f32[2,2048,2,512]{3,2,1,0:T(2,128)}, f32[2048,128]{1,0:T(8,128)})) %all-reduce.7.cloned.1.call-update) | async-done | bytes 18055184 | tf_op jit(solution)/shard_map/psum | solution.py:206
  1271.8 12.0 copy.107
  (287 shorter events, 376.0 us)
Async XLA Ops:
  7.2 155.5 %copy-start = (bf16[2048,128]{1,0:T(8,128)(2,1)S(1)}, bf16[2048,128]{1,0:T(8,128)(2,1)}, u32[]{:S(2)}) copy-start(bf16[2048,128]{1,0:T(8,128)(2,1)} %param.33) | copy-start | bytes 1572868
  7.2 142.3 %all-gather.4.cloned.1.call-start = ((), (), s32[]{:S(2)}) async-start(), calls=%async_computation.3 | async-start | bytes 5242880 | tf_op jit(solution)/shard_map/all_gather | solution.py:137
  112.2 85.1 %all-gather.6.cloned.1.call-start = ((), (), s32[]{:S(2)}) async-start(), calls=%async_computation.4 | async-start | bytes 5242880 | tf_op jit(solution)/shard_map/all_gather | solution.py:150
  162.6 109.5 %reduce-scatter.4.cloned.1.call-start = ((), (), s32[]{:S(2)}) async-start(), calls=%async_computation.6 | async-start | bytes 10485760 | tf_op jit(solution)/shard_map/reduce_scatter | solution.py:106
  167.4 192.4 %reduce-scatter.6.cloned.1.call-start = ((), (), s32[]{:S(2)}) async-start(), calls=%async_computation.7 | async-start | bytes 10485760 | tf_op jit(solution)/shard_map/reduce_scatter | solution.py:106
  287.8 124.9 %all-gather.8.cloned.1.call-start = ((), (), s32[]{:S(2)}) async-start(), calls=%async_computation.5 | async-start | bytes 5242880 | tf_op jit(solution)/shard_map/all_gather | solution.py:150
  288.4 181.9 %reduce-scatter.8.cloned.1.call-start = ((), (), s32[]{:S(2)}) async-start(), calls=%async_computation.8 | async-start | bytes 10485760 | tf_op jit(solution)/shard_map/reduce_scatter | solution.py:193
  363.8 53.8 %copy-start.8 = (bf16[1024,512]{0,1:T(8,128)(2,1)}, bf16[1024,512]{0,1:T(8,128)(2,1)S(1)}, u32[]{:S(2)}) copy-start(bf16[1024,512]{0,1:T(8,128)(2,1)S(1)} %get-tuple-element.490) | copy-start | bytes 3145732
  388.0 882.1 %all-reduce.7.cloned.1.call-start = ((), (), s32[]{:S(2)}) async-start(), calls=%async_computation.9 | async-start | bytes 36110336 | tf_op jit(solution)/shard_map/psum | solution.py:206
  450.9 21.2 %copy-start.27 = (bf16[262,16]{0,1:T(8,128)(2,1)S(1)}, bf16[262,16]{0,1:T(8,128)(2,1)}, u32[]{:S(2)}) copy-start(bf16[262,16]{0,1:T(8,128)(2,1)} %get-tuple-element.734) | copy-start | bytes 25156
  472.1 247.7 %copy-start.25 = (f32[7,512]{1,0:T(8,128)S(1)}, f32[7,512]{1,0:T(8,128)}, u32[]{:S(2)}) copy-start(f32[7,512]{1,0:T(8,128)} %get-tuple-element.495) | copy-start | bytes 43012
  475.3 10.7 copy-start.2
  486.0 16.0 %copy-start.1 = (f32[256,50,512]{2,0,1:T(8,128)S(1)}, f32[256,50,512]{2,0,1:T(8,128)}, u32[]{:S(2)}) copy-start(f32[256,50,512]{2,0,1:T(8,128)} %get-tuple-element.619) | copy-start | bytes 78643200 | tf_op jit(solution)/shard_map/while
  527.3 6.8 copy-start.24
  537.1 10.7 copy-start.2
  547.8 16.0 %copy-start.1 = (f32[256,50,512]{2,0,1:T(8,128)S(1)}, f32[256,50,512]{2,0,1:T(8,128)}, u32[]{:S(2)}) copy-start(f32[256,50,512]{2,0,1:T(8,128)} %get-tuple-element.619) | copy-start | bytes 78643200 | tf_op jit(solution)/shard_map/while
  589.1 6.8 copy-start.24
  598.9 10.7 copy-start.2
  609.6 16.0 %copy-start.1 = (f32[256,50,512]{2,0,1:T(8,128)S(1)}, f32[256,50,512]{2,0,1:T(8,128)}, u32[]{:S(2)}) copy-start(f32[256,50,512]{2,0,1:T(8,128)} %get-tuple-element.619) | copy-start | bytes 78643200 | tf_op jit(solution)/shard_map/while
  650.8 6.8 copy-start.24
  660.7 10.7 copy-start.2
  671.4 16.0 %copy-start.1 = (f32[256,50,512]{2,0,1:T(8,128)S(1)}, f32[256,50,512]{2,0,1:T(8,128)}, u32[]{:S(2)}) copy-start(f32[256,50,512]{2,0,1:T(8,128)} %get-tuple-element.619) | copy-start | bytes 78643200 | tf_op jit(solution)/shard_map/while
  712.6 6.8 copy-start.24
  1271.8 12.0 copy-start.22
  (27 other events, 104.3 us)
Sparse Core Ops, SparseCore 0:
  112.3 37.1 all-gather.3
  162.7 34.4 all-gather.5
  200.4 71.6 reduce-scatter.3
  287.9 71.7 reduce-scatter.5
  361.7 34.4 all-gather.7
  398.6 71.6 reduce-scatter.7
  720.6 549.5 all-reduce.6
where the time goes:
time: 1300 us; the launch traced here: 1290 us
  waiting for transfers between devices  657 us (51%)
  matrix products  254 us (20%)
  other arithmetic  176 us (14%)
  local copies, waits for them, and re-layouts  95.5 us (7%)
  blocking collectives  81 us (6%)
  between operations  14.9 us (1%)
    psum x1, waiting for transfers between devices, on_device(): lax.psum((conv_w_grad, conv_b_grad, high_w_grad, high_b_grad, proj_w_grad...  462 us
    reduce_scatter x2, waiting for transfers between devices, sum_features(): lax.psum_scatter(partial_value, 'mp', scatter_dimension=1, tiled=True)  125 us
    reduce_sum x8, other arithmetic, pool_weights(): denom_sum = jnp.sum(expo_terms, axis=1)  88.9 us
    dot_general x8, matrix products, conv_preact(): jnp.einsum('tpk,kf->tpf', unfolded, flat_w, preferred_element_type=jnp.fl...  85.3 us
    psum x1, blocking collectives, on_device(): embed_grad = lax.psum(embed_acc, ('dp', 'mp'))  42.1 us
    psum x1, blocking collectives, on_device(): lax.psum((conv_w_grad, conv_b_grad, high_w_grad, high_b_grad, proj_w_grad...  39 us
    dot_general x4, matrix products, one_block(): jnp.einsum('tpf,kf->tpk', pre_grad, flat_w, preferred_element_type=jnp.fl...  35.4 us
    convert_element_type x4, other arithmetic, one_block(): pre_grad = (weights * pool_grad[:, None, :]).astype(jnp.bfloat16)  34.2 us
  transfers between devices with their start and end apart: 7, of which 6 were waited for; matrix products, arithmetic and copies ran while one was open for 10% of the time, Pallas kernels for 0%

commit v1 on v0

v1 whole, which is shorter than its diff:
```python
import functools

import jax
import jax.numpy as jnp
from jax import lax
from jax.experimental import pallas as pl
from jax.experimental.pallas import tpu as pltpu
from jax.sharding import PartitionSpec as P

log2e = 1.4426950408889634
ln2 = 0.6931471805599453
neg_large = -1e30
f32 = jnp.float32
bf16 = jnp.bfloat16
vmem_bytes = 58 << 20


def widths_of(cols, full_width):
    widths = jnp.ones(cols.shape, jnp.int32)
    for divisor in (64, 32, 16, 8, 4, 2):
        widths = widths + (cols >= full_width // divisor).astype(jnp.int32)
    return widths


def sigmoid(v):
    return 1.0 / (1.0 + jnp.exp(-v))


def column_of(row):
    return jnp.transpose(jnp.broadcast_to(row, (8, row.shape[1])))[:, :1]


def params(**kw):
    return pltpu.CompilerParams(vmem_limit_bytes=vmem_bytes, **kw)


def cost(flops, nbytes):
    return pl.CostEstimate(flops=int(flops), bytes_accessed=int(nbytes), transcendentals=0)


def masked_taps(first, w_ref, char_dim, full_width):
    depth, filters = w_ref.shape
    cols = first + lax.broadcasted_iota(jnp.int32, (depth, filters), 1)
    taps = lax.broadcasted_iota(jnp.int32, (depth, filters), 0) // char_dim
    flat = jnp.where(taps < widths_of(cols, full_width), w_ref[...].astype(f32), 0.0)
    pad = (-depth) % 128
    return jnp.concatenate([flat, jnp.zeros((pad, filters), f32)], axis=0)


def split_taps(flat):
    scaled = jnp.transpose(flat) * log2e
    high = scaled.astype(bf16)
    low = (scaled - high.astype(f32)).astype(bf16)
    return jnp.concatenate([high, low], axis=1)


def last_place(first, filters, char_count, full_width):
    cols = first + lax.broadcasted_iota(jnp.int32, (filters, 128), 0)
    return char_count - widths_of(cols, full_width)


def embed_chars(ids_ref, tab_ref, cv_ref):
    char_count, tokens = ids_ref.shape
    char_dim = tab_ref.shape[0]
    for place in range(char_count):
        for block in range(tokens // 128):
            lanes = slice(block * 128, block * 128 + 128)
            ids = jnp.broadcast_to(ids_ref[place : place + 1, lanes], (8, 128))
            low, high = ids & 127, ids >> 7
            rows = []
            for part in range(char_dim // 8):
                found = None
                for tile in range(tab_ref.shape[1] // 128):
                    table = tab_ref[part * 8 : part * 8 + 8, tile * 128 : tile * 128 + 128]
                    got = jnp.take_along_axis(table, low, axis=1)
                    found = got if tile == 0 else jnp.where(high == tile, got, found)
                rows.append(found)
            cv_ref[place * char_dim : (place + 1) * char_dim, lanes] = jnp.concatenate(
                rows, axis=0
            ).astype(bf16)
    rest = char_count * char_dim
    cv_ref[rest:, :] = jnp.zeros((cv_ref.shape[0] - rest, tokens), bf16)


def conv_fwd_kernel(
    char_dim, taps, full_width,
    first_ref, ids_ref, tab_ref, w_ref, bias_ref,
    out_ref, pooled_ref, cv_ref,
    w2_ref, last_ref, bias_col_ref, peak_ref, sum_ref,
):
    char_count = ids_ref.shape[0]
    filters = w2_ref.shape[0]

    @pl.when(pl.program_id(0) == 0)
    def _():
        first = first_ref[0]
        w2_ref[...] = split_taps(masked_taps(first, w_ref, char_dim, full_width))
        last_ref[...] = last_place(first, filters, char_count, full_width)
        bias_col_ref[...] = jnp.broadcast_to(column_of(bias_ref[...].astype(f32)), bias_col_ref.shape)

    embed_chars(ids_ref, tab_ref, cv_ref)

    def scores(start):
        window = cv_ref[pl.ds(start, 128), :]
        return jnp.dot(
            w2_ref[...], jnp.concatenate([window, window], axis=0), preferred_element_type=f32
        )

    total = None
    for place in range(char_count):
        term = jnp.exp2(scores(place * char_dim))
        if place > char_count - taps:
            term = jnp.where(place <= last_ref[:, :1], term, 0.0)
        total = term if total is None else total + term
    sum_ref[...] = total
    peak_ref[...] = jnp.zeros_like(peak_ref)
    fine = jnp.logical_and(jnp.min(sum_ref[...]) > 1e-15, jnp.max(sum_ref[...]) < 1e15)

    @pl.when(jnp.logical_not(fine))
    def _():
        peak_ref[...] = jnp.full(peak_ref.shape, neg_large, f32)

        def shifted(place):
            got = scores(pl.multiple_of(place * char_dim, char_dim))
            return jnp.where(place <= last_ref[:, :1], got, neg_large)

        def find(place, carry):
            peak_ref[...] = jnp.maximum(peak_ref[...], shifted(place))
            return carry

        lax.fori_loop(0, char_count, find, 0)
        sum_ref[...] = jnp.zeros_like(sum_ref)

        def add(place, carry):
            sum_ref[...] += jnp.exp2(shifted(place) - peak_ref[...])
            return carry

        lax.fori_loop(0, char_count, add, 0)

    pooled = peak_ref[...] * ln2 + jnp.log(sum_ref[...])
    pooled_ref[...] = pooled
    v = pooled + bias_col_ref[:, :1]
    out_ref[...] = (v * sigmoid(v)).astype(bf16)


def conv_forward(first, ids_t, table, flat_w, bias_row, taps, full_width, start, tokens):
    char_count = ids_t.shape[0]
    char_dim = table.shape[0]
    depth, filters = flat_w.shape
    block = min(256, tokens)
    shift = start // block
    cv_rows = (char_count - 1) * char_dim + 128
    whole = lambda shape: pl.BlockSpec(shape, lambda i: (0, 0))
    by_block = lambda rows: pl.BlockSpec((rows, block), lambda i: (0, i))
    return pl.pallas_call(
        functools.partial(conv_fwd_kernel, char_dim, taps, full_width),
        grid=(tokens // block,),
        in_specs=[
            pl.BlockSpec(memory_space=pltpu.SMEM),
            pl.BlockSpec((char_count, block), lambda i: (0, i + shift)),
            whole(table.shape),
            whole(flat_w.shape),
            whole(bias_row.shape),
        ],
        out_specs=[by_block(filters), by_block(filters), by_block(cv_rows)],
        out_shape=[
            jax.ShapeDtypeStruct((filters, tokens), bf16),
            jax.ShapeDtypeStruct((filters, tokens), f32),
            jax.ShapeDtypeStruct((cv_rows, tokens), bf16),
        ],
        scratch_shapes=[
            pltpu.VMEM((filters, 256), bf16),
            pltpu.VMEM((filters, 128), jnp.int32),
            pltpu.VMEM((filters, 128), f32),
            pltpu.VMEM((filters, block), f32),
            pltpu.VMEM((filters, block), f32),
        ],
        compiler_params=params(),
        cost_estimate=cost(2 * tokens * char_count * 256 * filters, 8 * tokens * filters),
        name="conv_fwd",
    )(first, ids_t, table, flat_w, bias_row)


def conv_prep_kernel(char_dim, full_width, char_count, group, first_ref, w_ref, bias_ref,
                     w2_ref, spread_ref, last_ref, bias_col_ref):
    first = first_ref[0]
    depth, filters = w_ref.shape
    flat = masked_taps(first, w_ref, char_dim, full_width)
    w2_ref[...] = split_taps(flat)
    narrow = flat[:depth].astype(bf16)
    spread_ref[...] = jnp.zeros_like(spread_ref)
    for r in range(group):
        spread_ref[r * char_dim : r * char_dim + depth, r * filters : (r + 1) * filters] = narrow
    last_ref[...] = last_place(first, filters, char_count, full_width)
    bias_col_ref[...] = jnp.broadcast_to(column_of(bias_ref[...].astype(f32)), bias_col_ref.shape)


def conv_prep(first, flat_w, bias_row, char_dim, char_count, full_width, group):
    depth, filters = flat_w.shape
    vm = pl.BlockSpec(memory_space=pltpu.VMEM)
    return pl.pallas_call(
        functools.partial(conv_prep_kernel, char_dim, full_width, char_count, group),
        in_specs=[pl.BlockSpec(memory_space=pltpu.SMEM), vm, vm],
        out_specs=[vm] * 4,
        out_shape=[
            jax.ShapeDtypeStruct((filters, 256), bf16),
            jax.ShapeDtypeStruct((256, group * filters), bf16),
            jax.ShapeDtypeStruct((filters, 128), jnp.int32),
            jax.ShapeDtypeStruct((filters, 128), f32),
        ],
        compiler_params=params(),
        name="conv_prep",
    )(first, flat_w, bias_row)


def conv_bwd_kernel(
    char_dim, taps, group,
    ids_ref, cv_ref, w2_ref, spread_ref, last_ref, bias_ref, pooled_ref, part_ref, come_ref,
    dw_ref, de_ref, db_ref,
    dcv_ref, pool_grad_ref, shift_ref,
):
    char_count, tokens = ids_ref.shape
    vocab = de_ref.shape[0]

    @pl.when(pl.program_id(0) == 0)
    def _():
        dw_ref[...] = jnp.zeros_like(dw_ref)
        de_ref[...] = jnp.zeros_like(de_ref)
        db_ref[...] = jnp.zeros_like(db_ref)

    grad = (part_ref[...] + come_ref[...].astype(f32)).astype(bf16).astype(f32)
    pooled = pooled_ref[...]
    v = pooled + bias_ref[:, :1]
    sig = sigmoid(v)
    pool_grad = grad * sig * (1.0 + v * (1.0 - sig))
    pool_grad_ref[...] = pool_grad
    shift_ref[...] = pooled * log2e
    db_ref[...] += sum(pool_grad[:, k : k + 128] for k in range(0, tokens, 128))
    dcv_ref[...] = jnp.zeros_like(dcv_ref)
    symbols = lax.broadcasted_iota(jnp.int32, (vocab, tokens), 0)
    nt = (((1,), (1,)), ((), ()))

    def some_places(base, masked):
        windows, grads = [], []
        for k in range(group):
            window = cv_ref[pl.ds(pl.multiple_of((base + k) * char_dim, char_dim), 128), :]
            score = jnp.dot(
                w2_ref[...], jnp.concatenate([window, window], axis=0), preferred_element_type=f32
            )
            got = jnp.exp2(score - shift_ref[...]) * pool_grad_ref[...]
            if masked:
                got = jnp.where(base + k <= last_ref[:, :1], got, 0.0)
            windows.append(window)
            grads.append(got.astype(bf16))
        span = pl.ds(pl.multiple_of(base * char_dim, char_dim), 256)
        dcv_ref[span, :] += jnp.dot(
            spread_ref[...], jnp.concatenate(grads, axis=0), preferred_element_type=f32
        )
        dw_ref[...] += lax.dot_general(
            jnp.concatenate(grads, axis=1),
            jnp.concatenate(windows, axis=1),
            nt,
            preferred_element_type=f32,
        )
        onehots, sums = [], []
        for k in range(group):
            ids = jnp.broadcast_to(ids_ref[pl.ds(base + k, 1), :], (vocab, tokens))
            onehots.append(jnp.where(symbols == ids, 1.0, 0.0).astype(bf16))
            rows = pl.ds(pl.multiple_of((base + k) * char_dim, char_dim), char_dim)
            sums.append(dcv_ref[rows, :].astype(bf16))
        de_ref[...] += lax.dot_general(
            jnp.concatenate(onehots, axis=1),
            jnp.concatenate(sums, axis=1),
            nt,
            preferred_element_type=f32,
        )

    whole = (char_count - taps + 1) // group

    def step(i, carry):
        some_places(i * group, False)
        return carry

    lax.fori_loop(0, whole, step, 0)
    for i in range(whole, char_count // group):
        some_places(i * group, True)


def conv_backward(ids_t, cv, prepared, pooled, part, come, char_dim, taps, vocab, group, at, tokens, cv_at):
    w2, spread, last, bias = prepared
    char_count = ids_t.shape[0]
    filters = w2.shape[0]
    block = min(256, tokens)
    base, inner = at // block, (at - cv_at) // block
    whole = lambda a: pl.BlockSpec(a.shape, lambda i: (0, 0))
    by_block = lambda rows, shift: pl.BlockSpec((rows, block), lambda i: (0, i + shift))
    vocab_rows = -(-vocab // 16) * 16
    return pl.pallas_call(
        functools.partial(conv_bwd_kernel, char_dim, taps, group),
        grid=(tokens // block,),
        in_specs=[
            by_block(char_count, base),
            by_block(cv.shape[0], inner),
            whole(w2), whole(spread), whole(last), whole(bias),
            by_block(filters, inner),
            by_block(filters, base),
            by_block(filters, base),
        ],
        out_specs=[
            pl.BlockSpec((filters, 128), lambda i: (0, 0)),
            pl.BlockSpec((vocab_rows, char_dim), lambda i: (0, 0)),
            pl.BlockSpec((filters, 128), lambda i: (0, 0)),
        ],
        out_shape=[
            jax.ShapeDtypeStruct((filters, 128), f32),
            jax.ShapeDtypeStruct((vocab_rows, char_dim), f32),
            jax.ShapeDtypeStruct((filters, 128), f32),
        ],
        scratch_shapes=[
            pltpu.VMEM((cv.shape[0] + 16 * char_dim, block), f32),
            pltpu.VMEM((filters, block), f32),
            pltpu.VMEM((filters, block), f32),
        ],
        compiler_params=params(),
        cost_estimate=cost(2 * tokens * char_count * 896 * filters, 8 * tokens * filters),
        name="conv_bwd",
    )(ids_t, cv, w2, spread, last, bias, pooled, part, come)


def mixed_of(rank_ref, w_ref, bias_ref, piece_refs):
    total = None
    rows = piece_refs[0].shape[0]
    for k, piece in enumerate(piece_refs):
        at = pl.multiple_of((rank_ref[0] ^ k) * rows, rows)
        term = jnp.dot(w_ref[:, pl.ds(at, rows)], piece[...], preferred_element_type=f32)
        total = term if total is None else total + term
    return total + column_of(bias_ref[...].astype(f32))


def mix_grads(transform, gate, own, upstream):
    s, u = sigmoid(gate), sigmoid(transform)
    gate_grad = upstream * (own - transform * u) * s * (1.0 - s)
    trans_grad = upstream * (1.0 - s) * u * (1.0 + transform * (1.0 - u))
    return jnp.concatenate([trans_grad, gate_grad], axis=0).astype(bf16), s * upstream


def lane_sums(values):
    wide = values.astype(f32)
    return sum(wide[:, k : k + 128] for k in range(0, wide.shape[1], 128))


def lower_kernel(count, rank_ref, w_ref, bias_ref, *refs):
    pieces, (mixed_ref, next_ref) = refs[:count], refs[count:]
    mixed = mixed_of(rank_ref, w_ref, bias_ref, pieces)
    half = mixed.shape[0] // 2
    mixed_ref[...] = mixed
    transform, gate = mixed[:half], sigmoid(mixed[half:])
    update = gate * pieces[0][...].astype(f32) + (1.0 - gate) * transform * sigmoid(transform)
    next_ref[...] = update.astype(bf16)


def upper_kernel(count, rank_ref, w_ref, bias_ref, *refs):
    pieces, (grad_ref, next_ref, mix_ref, gated_ref, sums_ref) = refs[:count], refs[count:]
    mixed = mixed_of(rank_ref, w_ref, bias_ref, pieces)
    half = mixed.shape[0] // 2
    transform, gate = mixed[:half], mixed[half:]
    own = pieces[0][...].astype(f32)
    s = sigmoid(gate)
    next_ref[...] = (s * own + (1.0 - s) * transform * sigmoid(transform)).astype(bf16)
    mix, gated_ref[...] = mix_grads(transform, gate, own, grad_ref[...].astype(f32))
    mix_ref[...] = mix

    @pl.when(pl.program_id(0) == 0)
    def _():
        sums_ref[...] = jnp.zeros_like(sums_ref)

    sums_ref[...] += lane_sums(mix)


def highway(rank, weight, bias_row, pieces, upstream=None, at=0):
    columns, full = weight.shape
    half = columns // 2
    tokens = pieces[0].shape[1]
    block = min(256, tokens)
    count = len(pieces)
    rows = full // count
    whole = lambda shape: pl.BlockSpec(shape, lambda i: (0, 0))
    by_block = lambda r, shift=0: pl.BlockSpec((r, block), lambda i: (0, i + shift))
    in_specs = [pl.BlockSpec(memory_space=pltpu.SMEM), whole(weight.shape), whole(bias_row.shape)]
    in_specs += [by_block(rows)] * count
    args = [rank, weight, bias_row, *pieces]
    if upstream is None:
        kernel, name = lower_kernel, "highway_lower"
        out_specs = [by_block(columns), by_block(half)]
        out_shape = [
            jax.ShapeDtypeStruct((columns, tokens), f32),
            jax.ShapeDtypeStruct((half, tokens), bf16),
        ]
    else:
        kernel, name = upper_kernel, "highway_upper"
        in_specs.append(by_block(half, at // block))
        args.append(upstream)
        out_specs = [by_block(half), by_block(columns), by_block(half), whole((columns, 128))]
        out_shape = [
            jax.ShapeDtypeStruct((half, tokens), bf16),
            jax.ShapeDtypeStruct((columns, tokens), bf16),
            jax.ShapeDtypeStruct((half, tokens), f32),
            jax.ShapeDtypeStruct((columns, 128), f32),
        ]
    return pl.pallas_call(
        functools.partial(kernel, count),
        grid=(tokens // block,),
        in_specs=in_specs,
        out_specs=out_specs,
        out_shape=out_shape,
        compiler_params=params(),
        cost_estimate=cost(2 * tokens * columns * full, 2 * columns * full + 8 * columns * tokens),
        name=name,
    )(*args)


def mix_kernel(mixed_ref, own_ref, part_ref, come_ref, mix_ref, gated_ref, sums_ref):
    half = own_ref.shape[0]
    upstream = (part_ref[...] + come_ref[...].astype(f32)).astype(bf16).astype(f32)
    mix, gated_ref[...] = mix_grads(
        mixed_ref[:half], mixed_ref[half:], own_ref[...].astype(f32), upstream
    )
    mix_ref[...] = mix

    @pl.when(pl.program_id(0) == 0)
    def _():
        sums_ref[...] = jnp.zeros_like(sums_ref)

    sums_ref[...] += lane_sums(mix)


def mix_backward(mixed, own, part, come, at):
    columns, tokens = mixed.shape
    half = columns // 2
    block = min(256, tokens)
    by_block = lambda r, shift=0: pl.BlockSpec((r, block), lambda i: (0, i + shift))
    return pl.pallas_call(
        mix_kernel,
        grid=(tokens // block,),
        in_specs=[by_block(columns), by_block(half), by_block(half, at // block), by_block(half, at // block)],
        out_specs=[by_block(columns), by_block(half), pl.BlockSpec((columns, 128), lambda i: (0, 0))],
        out_shape=[
            jax.ShapeDtypeStruct((columns, tokens), bf16),
            jax.ShapeDtypeStruct((half, tokens), f32),
            jax.ShapeDtypeStruct((columns, 128), f32),
        ],
        compiler_params=params(),
        cost_estimate=cost(30 * columns * tokens, 8 * columns * tokens),
        name="mix_backward",
    )(mixed, own, part, come)


def weight_grad_kernel(count, rank_ref, *refs):
    features, mixes, out_ref = refs[:count], refs[count : 2 * count], refs[-1]
    total = None
    for a, b in zip(features, mixes):
        term = lax.dot_general(a[...], b[...], (((1,), (1,)), ((), ())), preferred_element_type=f32)
        total = term if total is None else total + term
    out_ref[...] = total.astype(bf16)


def weight_grad(rank, pieces, mixes):
    chunks, count = len(pieces), len(pieces[0])
    rows = pieces[0][0].shape[0]
    columns = mixes[0].shape[0]
    tokens = sum(m.shape[1] for m in mixes)
    outs = None
    for k in range(count):
        args = [rank, *[pieces[c][k] for c in range(chunks)], *mixes]
        specs = [pl.BlockSpec(memory_space=pltpu.SMEM)]
        block = rows // 2
        specs += [pl.BlockSpec((block, m.shape[1]), lambda i, r: (i, 0)) for m in mixes]
        specs += [pl.BlockSpec(m.shape, lambda i, r: (0, 0)) for m in mixes]
        outs = _weight_grad_part(args, specs[1:], chunks, k, rows, block, count * rows, columns, tokens, outs)
    return outs


def _weight_grad_part(args, specs, chunks, k, rows, block, full, columns, tokens, before):
    steps = rows // block

    def kernel(rank_ref, *refs):
        if before is not None:
            refs = refs[1:]
        weight_grad_kernel(chunks, rank_ref, *refs)

    alias = {}
    if before is not None:
        args = [args[0], before, *args[1:]]
        specs = [pl.BlockSpec(memory_space=pl.ANY), *specs]
        alias = {1: 0}
    return pl.pallas_call(
        kernel,
        grid_spec=pltpu.PrefetchScalarGridSpec(
            num_scalar_prefetch=1,
            grid=(steps,),
            in_specs=specs,
            out_specs=pl.BlockSpec((block, columns), lambda i, r: ((r[0] ^ k) * steps + i, 0)),
        ),
        out_shape=jax.ShapeDtypeStruct((full, columns), bf16),
        input_output_aliases=alias,
        compiler_params=params(),
        cost_estimate=cost(2 * rows * columns * tokens, 2 * (rows * columns + (rows + columns) * tokens)),
        name="weight_grad",
    )(*args)


def input_grad_kernel(count, block, rank_ref, w_ref, mix_ref, gated_ref, *outs):
    for k, out in enumerate(outs):
        at = pl.multiple_of((rank_ref[0] ^ k) * block, block)
        got = jnp.dot(w_ref[pl.ds(at, block), :], mix_ref[...], preferred_element_type=f32)
        if k == 0:
            got = got + gated_ref[...]
        out[...] = got.astype(out.dtype)


def input_grad(rank, weight, mix, gated, count):
    full, columns = weight.shape
    rows = full // count
    tokens = mix.shape[1]
    block = min(256, tokens)
    by_block = lambda r: pl.BlockSpec((r, block), lambda i: (0, i))
    kinds = [bf16 if k % 2 else f32 for k in range(count)]
    return pl.pallas_call(
        functools.partial(input_grad_kernel, count, rows),
        grid=(tokens // block,),
        in_specs=[
            pl.BlockSpec(memory_space=pltpu.SMEM),
            pl.BlockSpec(weight.shape, lambda i: (0, 0)),
            by_block(columns),
            by_block(rows),
        ],
        out_specs=[by_block(rows)] * count,
        out_shape=[jax.ShapeDtypeStruct((rows, tokens), kind) for kind in kinds],
        compiler_params=params(),
        cost_estimate=cost(2 * tokens * columns * full, 2 * columns * full + 16 * rows * tokens),
        name="input_grad",
    )(rank, weight, mix, gated)


def swap(value, axis, size, offset):
    return lax.ppermute(value, axis, [(j, j ^ offset) for j in range(size)])


def gather_pieces(own, size):
    pieces = {0: own}
    offset = size // 2
    while offset:
        pieces.update({k ^ offset: swap(v, "mp", size, offset) for k, v in list(pieces.items())})
        offset //= 2
    return [pieces[k] for k in range(size)]


def scatter_sums(pieces, size):
    held = dict(enumerate(pieces))
    offset = 1
    while offset < size:
        stay = [k for k in held if not k & offset]
        come = {k: swap(held[k ^ offset].astype(bf16), "mp", size, offset) for k in stay}
        if len(stay) == 1:
            return held[0], come[0]
        held = {k: held[k].astype(f32) + come[k].astype(f32) for k in stay}
        offset *= 2
    return held[0], jnp.zeros(held[0].shape, bf16)


class Ring:
    def __init__(self, size):
        self.size = size
        order = list(range(0, size, 2)) + list(range(1, size, 2))[::-1]
        up = [(order[i], order[(i + 1) % size]) for i in range(size)]
        self.perms = (up, [(b, a) for a, b in up])
        index = lax.axis_index("dp")
        self.place = jnp.where(index % 2 == 0, index // 2, size - 1 - index // 2)

    def chunk(self, way, steps):
        return lax.rem(self.place + (-steps if way == 0 else steps) + 4 * self.size, self.size)

    def reduce_scatter(self, value):
        rows = value.shape[0] // (2 * self.size)

        def local(way, steps):
            at = (way * self.size + self.chunk(way, steps)) * rows
            return lax.dynamic_slice_in_dim(value, at, rows, 0)

        out = []
        for way in (0, 1):
            moving = local(way, 1)
            for step in range(self.size - 1):
                came = lax.ppermute(moving, "dp", self.perms[way])
                moving = (came.astype(f32) + local(way, step + 2).astype(f32)).astype(bf16)
            out.append(moving)
        return out

    def all_gather(self, owned):
        found = []
        for way in (0, 1):
            moving = owned[way]
            for step in range(self.size):
                found.append((step, way * self.size + self.chunk(way, step), moving))
                if step < self.size - 1:
                    moving = lax.ppermute(moving, "dp", self.perms[way])
        return [(at, piece) for _, at, piece in sorted(found, key=lambda item: item[0])]


def all_sum(value, axis, size):
    offset = 1
    while offset < size:
        value = value + swap(value, axis, size, offset)
        offset *= 2
    return value


def on_device(
    dp,
    mp,
    char_ids,
    embedding,
    conv_weight,
    conv_bias,
    highway_weight,
    highway_bias,
    proj_weight,
    proj_bias,
    cotangent,
):
    taps, char_dim, filters = conv_weight.shape
    levels, full_width, _, columns = highway_weight.shape
    tokens, char_count = char_ids.shape
    vocab = embedding.shape[0]
    out_cols = proj_weight.shape[1]
    group = 10
    chunks = 2
    size = tokens // chunks
    rank = lax.axis_index("mp").astype(jnp.int32)
    rank_arr = rank.reshape(1)
    first = (rank * filters).reshape(1)
    ring = Ring(dp)

    ids_t = char_ids.T
    lanes = -(-vocab // 128) * 128
    table = jnp.pad(embedding.T.astype(f32), ((0, 0), (0, lanes - vocab)))
    flat_w = conv_weight.reshape(taps * char_dim, filters)
    bias_row = conv_bias.reshape(1, filters)

    cot_pieces = gather_pieces(cotangent, mp)
    proj_pieces = []
    for k in range(mp):
        rows = lax.dynamic_slice_in_dim(proj_weight, (rank ^ k) * filters, filters, 0)
        proj_pieces.append(rows if k == 0 else swap(rows, "mp", mp, k))
    top_grad = sum(
        lax.dot_general(a, b, (((1,), (1,)), ((), ())), preferred_element_type=f32)
        for a, b in zip(proj_pieces, cot_pieces)
    ).astype(bf16)

    convs = [
        conv_forward(first, ids_t, table, flat_w, bias_row, taps, full_width, c * size, size)
        for c in range(chunks)
    ]
    pieces = [[gather_pieces(convs[c][0], mp) for c in range(chunks)]]
    weights_t = [
        jnp.transpose(highway_weight[l], (1, 2, 0)).reshape(2 * columns, full_width)
        for l in range(levels)
    ]
    weights_n = [highway_weight[l].reshape(full_width, 2 * columns) for l in range(levels)]
    bias_rows = [highway_bias[l].reshape(1, 2 * columns) for l in range(levels)]
    kept = []
    for l in range(levels - 1):
        done = [highway(rank_arr, weights_t[l], bias_rows[l], pieces[l][c]) for c in range(chunks)]
        kept.append([mixed for mixed, _ in done])
        pieces.append([gather_pieces(out, mp) for _, out in done])
    top = levels - 1
    done = [
        highway(rank_arr, weights_t[top], bias_rows[top], pieces[top][c], top_grad, c * size)
        for c in range(chunks)
    ]
    last = jnp.concatenate([d[0] for d in done], axis=1)
    mixes = [d[1] for d in done]
    gated = [d[2] for d in done]
    bias_sums = [None] * levels
    bias_sums[top] = sum(d[3] for d in done)
    w_grads = [None] * levels
    w_grads[top] = weight_grad(rank_arr, pieces[top], mixes)

    prepared = conv_prep(first, flat_w, bias_row, char_dim, char_count, full_width, group)
    for l in range(top, -1, -1):
        parts = [input_grad(rank_arr, weights_n[l], mixes[c], gated[c], mp) for c in range(chunks)]
        joined = [jnp.concatenate([p[k] for p in parts], axis=1) for k in range(mp)]
        part, come = scatter_sums(joined, mp)
        if l == 0:
            break
        done = [
            mix_backward(kept[l - 1][c], pieces[l - 1][c][0], part, come, c * size)
            for c in range(chunks)
        ]
        mixes = [d[0] for d in done]
        gated = [d[1] for d in done]
        bias_sums[l - 1] = sum(d[2] for d in done)
        w_grads[l - 1] = weight_grad(rank_arr, pieces[l - 1], mixes)

    vector_parts = [
        lax.dot_general(last, p, (((0,), (0,)), ((), ())), preferred_element_type=f32)
        for p in proj_pieces
    ]
    vector_part, vector_come = scatter_sums(vector_parts, mp)
    token_vectors = (
        vector_part + vector_come.astype(f32) + proj_bias.astype(f32)[None, :]
    ).astype(bf16)
    proj_grads = []
    for k in range(mp):
        got = jnp.dot(last, cot_pieces[k], preferred_element_type=f32).astype(bf16)
        proj_grads.append(got if k == 0 else swap(got, "mp", mp, k))
    proj_grad = jnp.zeros((mp, filters, out_cols), bf16)
    for k in range(mp):
        proj_grad = lax.dynamic_update_slice(proj_grad, proj_grads[k][None], (rank ^ k, 0, 0))
    proj_grad = proj_grad.reshape(full_width, out_cols)

    high_w_grad = jnp.zeros((levels, full_width, 2, columns), f32)
    proj_w_grad = jnp.zeros((full_width, out_cols), f32)
    for l in range(top, -1, -1):
        value = w_grads[l]
        if l == 0:
            value = jnp.concatenate([value, proj_grad], axis=1)
        rows = full_width // (2 * dp)
        for at, piece in ring.all_gather(ring.reduce_scatter(value)):
            wide = piece.astype(f32)
            high_w_grad = lax.dynamic_update_slice(
                high_w_grad,
                wide[:, : 2 * columns].reshape(1, rows, 2, columns),
                (l, at * rows, 0, 0),
            )
            if l == 0:
                proj_w_grad = lax.dynamic_update_slice(
                    proj_w_grad, wide[:, 2 * columns :], (at * rows, 0)
                )

    run = min(256, tokens)
    sums = None
    for at in range(0, tokens, run):
        c = at // size
        got = conv_backward(
            ids_t, convs[c][2], prepared, convs[c][1], part, come,
            char_dim, taps, vocab, group, at, run, c * size,
        )
        sums = got if sums is None else [a + b for a, b in zip(sums, got)]
    dw, de, db = sums
    depth = taps * char_dim
    small = jnp.concatenate(
        [
            dw[:, :depth].T.reshape(-1),
            jnp.sum(db, axis=1),
            *[jnp.sum(s, axis=1) for s in bias_sums],
            jnp.sum(cotangent.astype(f32), axis=0),
            de[:vocab].T.reshape(-1),
        ]
    )
    small = all_sum(jnp.pad(small, (0, (-small.shape[0]) % 1024)).reshape(-1, 128), "dp", dp).reshape(-1)
    cuts = []
    at = 0
    for amount in (depth * filters, filters, *[2 * columns] * levels, out_cols, vocab * char_dim):
        cuts.append(small[at : at + amount])
        at += amount
    conv_w_grad = cuts[0].reshape(taps, char_dim, filters)
    conv_b_grad = cuts[1]
    high_b_grad = jnp.stack(cuts[2 : 2 + levels]).reshape(levels, 2, columns)
    proj_b_grad = cuts[2 + levels]
    embed_grad = all_sum(cuts[3 + levels].reshape(char_dim, vocab), "mp", mp).T
    cols = first[0] + jnp.arange(filters, dtype=jnp.int32)
    tap_ok = jnp.arange(taps)[:, None] < widths_of(cols, full_width)[None, :]
    conv_w_grad = jnp.where(tap_ok[:, None, :], conv_w_grad, 0.0)
    return (
        token_vectors,
        embed_grad,
        conv_w_grad,
        conv_b_grad,
        high_w_grad,
        high_b_grad,
        proj_w_grad,
        proj_b_grad,
    )


def solution(mesh):
    in_specs = (
        P("dp", None),
        P(),
        P(None, None, "mp"),
        P("mp"),
        P(None, None, None, "mp"),
        P(None, None, "mp"),
        P(None, "mp"),
        P("mp"),
        P("dp", "mp"),
    )
    out_specs = (
        P("dp", "mp"),
        P(),
        P(None, None, "mp"),
        P("mp"),
        P(None, None, None, "mp"),
        P(None, None, "mp"),
        P(None, "mp"),
        P("mp"),
    )
    return jax.shard_map(
        functools.partial(on_device, mesh.shape["dp"], mesh.shape["mp"]),
        mesh=mesh,
        in_specs=in_specs,
        out_specs=out_specs,
        check_vma=False,
    )
```

time: 1300 us -> 608 us (0.47)
  waiting for transfers between devices: 657 us -> 118 us
  matrix products: 254 us -> 10.6 us
  Pallas kernels: 0 us -> 191 us
  other arithmetic: 176 us -> 51.5 us
  blocking collectives: 81 us -> 0 us
  starting transfers between devices: 11.6 us -> 71.4 us
  local copies, waits for them, and re-layouts: 95.5 us -> 153 us
    psum x1 -> x0, waiting for transfers between devices: 462 us -> none  [on_device(): lax.psum((conv_w_grad, conv_b_grad, high_w_grad, high_b_grad, proj_w_grad...]
    dot_general x37 -> x12, matrix products: 254 us -> 10.6 us  [the longest x4 5.96 us: on_device(): lax.dot_general(last, p, (((0,), (0,)), ((), ())), preferred_element_type...]
    pallas_call x0 -> x25, Pallas kernels: none -> 191 us  [the longest x4 72 us: conv_backward(): pl.pallas_call(functools.partial(conv_bwd_kernel, char_dim, taps, group),...]
    reduce_scatter x3 -> x0, waiting for transfers between devices: 145 us -> none  [the longest x2 125 us: sum_features(): lax.psum_scatter(partial_value, 'mp', scatter_dimension=1, tiled=True)]
    ppermute x0 -> x91, waiting for transfers between devices: none -> 118 us  [the longest x28 48.7 us: reduce_scatter(): came = lax.ppermute(moving, 'dp', self.perms[way])]
    reduce_sum x15 -> x4, other arithmetic: 96.7 us -> 3.11 us  [the longest x2 1.62 us: on_device(): jnp.sum(s, axis=1)]
    psum x2 -> x0, blocking collectives: 81 us -> none  [the longest x1 42.1 us: on_device(): embed_grad = lax.psum(embed_acc, ('dp', 'mp'))]
    ppermute x0 -> x91, starting transfers between devices: none -> 71.4 us  [the longest x28 29.9 us: all_gather(): moving = lax.ppermute(moving, 'dp', self.perms[way])]
  transfers between devices with their start and end apart: 7 -> 91, of which waited for: 6 -> 37; matrix products, arithmetic and copies ran while one was open for 10% -> 31% of each run, Pallas kernels for 0% -> 29%
where the time goes in v1:
time: 608 us; the launch traced here: 597 us
  Pallas kernels  191 us (31%)
  local copies, waits for them, and re-layouts  153 us (25%)
  waiting for transfers between devices  118 us (19%)
  starting transfers between devices  71.4 us (12%)
  other arithmetic  51.5 us (8%)
  matrix products  10.6 us (2%)
    pallas_call x4, Pallas kernels, conv_backward(): pl.pallas_call(functools.partial(conv_bwd_kernel, char_dim, taps, group),...  72 us
    ppermute x28, waiting for transfers between devices, reduce_scatter(): came = lax.ppermute(moving, 'dp', self.perms[way])  48.7 us
    ppermute x28, waiting for transfers between devices, all_gather(): moving = lax.ppermute(moving, 'dp', self.perms[way])  41 us
    reshape x32, local copies, waits for them, and re-layouts, on_device(): wide[:, :2 * columns].reshape(1, rows, 2, columns)  39.3 us
    pallas_call x8, Pallas kernels, _weight_grad_part(): pl.pallas_call(kernel, grid_spec=pltpu.PrefetchScalarGridSpec(num_scalar_...  32.5 us
    ppermute x28, starting transfers between devices, all_gather(): moving = lax.ppermute(moving, 'dp', self.perms[way])  29.9 us
    dynamic_update_slice x32, local copies, waits for them, and re-layouts, on_device(): lax.dynamic_update_slice(high_w_grad, wide[:, :2 * columns].reshape(1, ro...  29.7 us
    ppermute x35, waiting for transfers between devices, swap(): return lax.ppermute(value, axis, [(j, j ^ offset) for j in range(size)])  28.7 us
  transfers between devices with their start and end apart: 91, of which 37 were waited for; matrix products, arithmetic and copies ran while one was open for 31% of the time, Pallas kernels for 29%

profile of v1, /device:TPU:0, one launch (start us, length us, event | category | flops | bytes accessed | tf_op | source)
XLA Modules:
  0.0 597.3 jit_solution(4852801903807211602)
XLA Ops:
  3.2 11.2 %conv_fwd.2 = (bf16[512,512]{1,0:T(8,128)(2,1)}, f32[512,512]{1,0:T(8,128)}, bf16[912,512]{1,0:T(8,128)(2,1)}) custom-call(s32[1]{0:T(128)} %bitcast.7.first_ref, s32[50,1024]{1,0:T(8,128)} %bitcast.114, f32[16,384]{1,0:T(8,128)} %pad_convert_fusion.tab_ref, bf16[112,512]{1,0:T(8,128)(2,1)} %bitcast.106, bf16[1,512]{1,0:T(2,128)(2,1)} %reshape.257.bias_ref), custom_call_target="tpu_custom_call" | custom-call | flops 6710886400 | bytes 2097152 | tf_op jit(solution)/shard_map/conv_fwd/pallas_call | solution.py:155
  17.5 11.3 %conv_fwd.3 = (bf16[512,512]{1,0:T(8,128)(2,1)}, f32[512,512]{1,0:T(8,128)}, bf16[912,512]{1,0:T(8,128)(2,1)}) custom-call(s32[1]{0:T(128)} %bitcast.7.first_ref, s32[50,1024]{1,0:T(8,128)} %bitcast.115, f32[16,384]{1,0:T(8,128)} %pad_convert_fusion.tab_ref, bf16[112,512]{1,0:T(8,128)(2,1)} %bitcast.107, bf16[1,512]{1,0:T(2,128)(2,1)} %reshape.257.bias_ref), custom_call_target="tpu_custom_call" | custom-call | flops 6710886400 | bytes 2097152 | tf_op jit(solution)/shard_map/conv_fwd/pallas_call | solution.py:155
  31.1 12.8 %fusion.40 = (bf16[1,2048,2,512]{3,2,1,0:T(2,128)(2,1)}, bf16[2,512,2048]{1,0,2:T(2,128)(2,1)}, bf16[2,512,2048]{1,0,2:T(2,128)(2,1)}, bf16[1,2048,2,512]{3,2,1,0:T(2,128)(2,1)}) fusion(bf16[2,2048,2,512]{3,2,1,0:T(2,128)(2,1)} %param.13), kind=kLoop, calls=%fused_computation.189 | loop fusion | bytes 25165824 | tf_op jit(solution)/shard_map/slice | solution.py:666
  44.2 11.2 %copy.26 = bf16[2,512,2048]{2,1,0:T(8,128)(2,1)} copy(bf16[2,512,2048]{1,0,2:T(2,128)(2,1)} %get-tuple-element.126) | data formatting | bytes 8388608 | tf_op jit(solution)/shard_map/transpose | solution.py:666
  57.7 6.6 %highway_lower.2 = (f32[1024,512]{1,0:T(8,128)}, bf16[512,512]{1,0:T(8,128)(2,1)}) custom-call(s32[1]{0:T(128)} %bitcast.rank_ref, bf16[1024,2048]{1,0:T(8,128)(2,1)} %bitcast.97, bf16[1,1024]{1,0:T(2,128)(2,1)} %bitcast.110, bf16[512,512]{1,0:T(8,128)(2,1)} %get-tuple-element.64.refs_0_.own_ref, bf16[512,512]{1,0:T(8,128)(2,1)} %collective-permute-done.refs_1_, ...), custom_call_target="tpu_custom_call" | custom-call | flops 2147483648 | bytes 8388608 | tf_op jit(solution)/shard_map/highway_lower/pallas_call | solution.py:410
  68.2 11.2 %copy.25 = bf16[2,512,2048]{2,1,0:T(8,128)(2,1)} copy(bf16[2,512,2048]{1,0,2:T(2,128)(2,1)} %get-tuple-element.125) | data formatting | bytes 8388608 | tf_op jit(solution)/shard_map/transpose | solution.py:666
  79.9 5.7 copy.31
  90.6 6.6 %highway_lower.3 = (f32[1024,512]{1,0:T(8,128)}, bf16[512,512]{1,0:T(8,128)(2,1)}) custom-call(s32[1]{0:T(128)} %bitcast.rank_ref, bf16[1024,2048]{1,0:T(8,128)(2,1)} %bitcast.98, bf16[1,1024]{1,0:T(2,128)(2,1)} %bitcast.111, bf16[512,512]{1,0:T(8,128)(2,1)} %get-tuple-element.67.refs_0_.own_ref.refs_1_, ...), custom_call_target="tpu_custom_call" | custom-call | flops 2147483648 | bytes 8388608 | tf_op jit(solution)/shard_map/highway_lower/pallas_call | solution.py:410
  103.7 10.8 %collective-permute-done.16.refs_2_ = bf16[512,512]{1,0:T(8,128)(2,1)S(1)} collective-permute-done((bf16[512,512]{1,0:T(8,128)(2,1)}, bf16[512,512]{1,0:T(8,128)(2,1)S(1)}, u32[]{:S(2)}, u32[]{:S(2)}) %collective-permute-start.16) | collective-permute-done | bytes 524320 | tf_op jit(solution)/shard_map/ppermute | solution.py:546
  117.0 7.6 %highway_upper.2 = (bf16[512,512]{1,0:T(8,128)(2,1)}, bf16[1024,512]{1,0:T(8,128)(2,1)}, f32[512,512]{1,0:T(8,128)}, f32[1024,128]{1,0:T(8,128)}) custom-call(s32[1]{0:T(128)} %bitcast.rank_ref, bf16[1024,2048]{1,0:T(8,128)(2,1)} %bitcast.101, bf16[1,1024]{1,0:T(2,128)(2,1)} %bitcast.112, bf16[512,512]{1,0:T(8,128)(2,1)} %get-tuple-element.65.refs_0_, ...), custom_call_target="tpu_custom_call" | custom-call | flops 2147483648 | bytes 8388608 | tf_op jit(solution)/shard_map/highway_upper/pallas_call | solution.py:410
  125.8 7.8 %highway_upper.3 = (bf16[512,512]{1,0:T(8,128)(2,1)}, bf16[1024,512]{1,0:T(8,128)(2,1)}, f32[512,512]{1,0:T(8,128)}, f32[1024,128]{1,0:T(8,128)}) custom-call(s32[1]{0:T(128)} %bitcast.rank_ref, bf16[1024,2048]{1,0:T(8,128)(2,1)} %bitcast.102, bf16[1,1024]{1,0:T(2,128)(2,1)} %bitcast.113, bf16[512,512]{1,0:T(8,128)(2,1)} %get-tuple-element.68.refs_0_.refs_1_, ...), custom_call_target="tpu_custom_call" | custom-call | flops 2147483648 | bytes 8388608 | tf_op jit(solution)/shard_map/highway_upper/pallas_call | solution.py:410
  141.7 6.1 %input_grad.5 = (f32[512,512]{1,0:T(8,128)}, bf16[512,512]{1,0:T(8,128)(2,1)}, f32[512,512]{1,0:T(8,128)}, bf16[512,512]{1,0:T(8,128)(2,1)}) custom-call(s32[1]{0:T(128)} %bitcast.rank_ref, bf16[2048,1024]{1,0:T(8,128)(2,1)} %bitcast.99, bf16[1024,512]{1,0:T(8,128)(2,1)} %get-tuple-element.80.mix_ref.refs_3_.refs_4_, f32[512,512]{1,0:T(8,128)} %get-tuple-element.81.gated_ref), custom_call_target="tpu_custom_call" | custom-call | flops 2147483648 | bytes 8388608 | tf_op jit(solution)/shard_map/input_grad/pallas_call | solution.py:528
  147.8 6.1 %input_grad.4 = (f32[512,512]{1,0:T(8,128)}, bf16[512,512]{1,0:T(8,128)(2,1)}, f32[512,512]{1,0:T(8,128)}, bf16[512,512]{1,0:T(8,128)(2,1)}) custom-call(s32[1]{0:T(128)} %bitcast.rank_ref, bf16[2048,1024]{1,0:T(8,128)(2,1)} %bitcast.100, bf16[1024,512]{1,0:T(8,128)(2,1)} %get-tuple-element.77.mix_ref.refs_2_.refs_3_, f32[512,512]{1,0:T(8,128)} %get-tuple-element.78.gated_ref), custom_call_target="tpu_custom_call" | custom-call | flops 2147483648 | bytes 8388608 | tf_op jit(solution)/shard_map/input_grad/pallas_call | solution.py:528
  235.0 6.1 %broadcast_in_dim.43 = f32[2,2048,2,512]{3,2,1,0:T(2,128)} broadcast(f32[]{:T(128)} %constant.119.clone.1), dimensions={} | broadcast | bytes 16777220 | tf_op jit(solution)/shard_map/broadcast_in_dim | solution.py:722
  270.4 6.1 %input_grad.7 = (f32[512,512]{1,0:T(8,128)}, bf16[512,512]{1,0:T(8,128)(2,1)}, f32[512,512]{1,0:T(8,128)}, bf16[512,512]{1,0:T(8,128)(2,1)}) custom-call(s32[1]{0:T(128)} %bitcast.rank_ref, bf16[2048,1024]{1,0:T(8,128)(2,1)} %bitcast.95, bf16[1024,512]{1,0:T(8,128)(2,1)} %get-tuple-element.93.mix_ref.refs_3_.refs_4_, f32[512,512]{1,0:T(8,128)} %get-tuple-element.94.gated_ref), custom_call_target="tpu_custom_call" | custom-call | flops 2147483648 | bytes 8388608 | tf_op jit(solution)/shard_map/input_grad/pallas_call | solution.py:528
  276.5 6.2 %input_grad.6 = (f32[512,512]{1,0:T(8,128)}, bf16[512,512]{1,0:T(8,128)(2,1)}, f32[512,512]{1,0:T(8,128)}, bf16[512,512]{1,0:T(8,128)(2,1)}) custom-call(s32[1]{0:T(128)} %bitcast.rank_ref, bf16[2048,1024]{1,0:T(8,128)(2,1)} %bitcast.96, bf16[1024,512]{1,0:T(8,128)(2,1)} %get-tuple-element.89.mix_ref.refs_2_.refs_3_, f32[512,512]{1,0:T(8,128)} %get-tuple-element.90.gated_ref), custom_call_target="tpu_custom_call" | custom-call | flops 2147483648 | bytes 8388608 | tf_op jit(solution)/shard_map/input_grad/pallas_call | solution.py:528
  351.4 8.4 %collective-permute-done.26.come_ref = bf16[512,1024]{1,0:T(8,128)(2,1)} collective-permute-done((bf16[512,1024]{1,0:T(8,128)(2,1)}, bf16[512,1024]{1,0:T(8,128)(2,1)}, u32[]{:S(2)}, u32[]{:S(2)}) %collective-permute-start.26) | collective-permute-done | bytes 1048608 | tf_op jit(solution)/shard_map/ppermute | solution.py:546
  359.7 17.8 %conv_bwd.7 = (f32[512,128]{1,0:T(8,128)}, f32[272,16]{1,0:T(8,128)}, f32[512,128]{1,0:T(8,128)}) custom-call(s32[50,1024]{1,0:T(8,128)} %bitcast.116, bf16[912,512]{1,0:T(8,128)(2,1)} %get-tuple-element.104.cv_ref, bf16[512,256]{1,0:T(8,128)(2,1)} %get-tuple-element.71.w2_ref, bf16[256,5120]{1,0:T(8,128)(2,1)} %get-tuple-element.72.spread_ref, ...), custom_call_target="tpu_custom_call" | custom-call | flops 11744051200 | bytes 1048576 | tf_op jit(solution)/shard_map/conv_bwd/pallas_call | solution.py:298
  377.6 18.3 %conv_bwd.6 = (f32[512,128]{1,0:T(8,128)}, f32[272,16]{1,0:T(8,128)}, f32[512,128]{1,0:T(8,128)}) custom-call(s32[50,1024]{1,0:T(8,128)} %bitcast.117, bf16[912,512]{1,0:T(8,128)(2,1)} %get-tuple-element.104.cv_ref, bf16[512,256]{1,0:T(8,128)(2,1)} %get-tuple-element.71.w2_ref, bf16[256,5120]{1,0:T(8,128)(2,1)} %get-tuple-element.72.spread_ref, ...), custom_call_target="tpu_custom_call" | custom-call | flops 11744051200 | bytes 1048576 | tf_op jit(solution)/shard_map/conv_bwd/pallas_call | solution.py:298
  395.8 17.8 %conv_bwd.5 = (f32[512,128]{1,0:T(8,128)}, f32[272,16]{1,0:T(8,128)}, f32[512,128]{1,0:T(8,128)}) custom-call(s32[50,1024]{1,0:T(8,128)} %bitcast.118, bf16[912,512]{1,0:T(8,128)(2,1)} %get-tuple-element.70.cv_ref, bf16[512,256]{1,0:T(8,128)(2,1)} %get-tuple-element.71.w2_ref, bf16[256,5120]{1,0:T(8,128)(2,1)} %get-tuple-element.72.spread_ref, ...), custom_call_target="tpu_custom_call" | custom-call | flops 11744051200 | bytes 1048576 | tf_op jit(solution)/shard_map/conv_bwd/pallas_call | solution.py:298
  413.7 18.1 %conv_bwd.4 = (f32[512,128]{1,0:T(8,128)}, f32[272,16]{1,0:T(8,128)}, f32[512,128]{1,0:T(8,128)}) custom-call(s32[50,1024]{1,0:T(8,128)} %bitcast.119, bf16[912,512]{1,0:T(8,128)(2,1)} %get-tuple-element.70.cv_ref, bf16[512,256]{1,0:T(8,128)(2,1)} %get-tuple-element.71.w2_ref, bf16[256,5120]{1,0:T(8,128)(2,1)} %get-tuple-element.72.spread_ref, ...), custom_call_target="tpu_custom_call" | custom-call | flops 11744051200 | bytes 1048576 | tf_op jit(solution)/shard_map/conv_bwd/pallas_call | solution.py:298
  545.1 6.1 %collective-permute-done.81 = bf16[128,1152]{1,0:T(8,128)(2,1)S(1)} collective-permute-done((bf16[128,1152]{1,0:T(8,128)(2,1)S(1)}, bf16[128,1152]{1,0:T(8,128)(2,1)S(1)}, u32[]{:S(2)}, u32[]{:S(2)}) %collective-permute-start.81) | collective-permute-done | bytes 294944 | tf_op jit(solution)/shard_map/ppermute | solution.py:606
  555.4 7.3 %collective-permute-done.83 = bf16[128,1152]{1,0:T(8,128)(2,1)S(1)} collective-permute-done((bf16[128,1152]{1,0:T(8,128)(2,1)S(1)}, bf16[128,1152]{1,0:T(8,128)(2,1)S(1)}, u32[]{:S(2)}, u32[]{:S(2)}) %collective-permute-start.83) | collective-permute-done | bytes 294944 | tf_op jit(solution)/shard_map/ppermute | solution.py:606
  567.1 6.7 %collective-permute-done.85 = bf16[128,1152]{1,0:T(8,128)(2,1)S(1)} collective-permute-done((bf16[128,1152]{1,0:T(8,128)(2,1)S(1)}, bf16[128,1152]{1,0:T(8,128)(2,1)S(1)}, u32[]{:S(2)}, u32[]{:S(2)}) %collective-permute-start.85) | collective-permute-done | bytes 294944 | tf_op jit(solution)/shard_map/ppermute | solution.py:606
  (480 shorter events, 361.4 us)
Async XLA Ops:
  14.4 43.2 %collective-permute-start = (bf16[512,512]{1,0:T(8,128)(2,1)}, bf16[512,512]{1,0:T(8,128)(2,1)}, u32[]{:S(2)}, u32[]{:S(2)}) collective-permute-start(bf16[512,512]{1,0:T(8,128)(2,1)} %get-tuple-element.64.refs_0_.own_ref), channel_id=1, source_target_pairs={{0,1},{1,0},{2,3},{3,2},{4,5},{5,4},{6,7},{7,6},{8,9},{9,8},{10,11... | collective-permute-start | bytes 1572872 | tf_op jit(solution)/shard_map/ppermute | solution.py:546
  15.0 29.1 %collective-permute-start.1 = (bf16[512,512]{1,0:T(8,128)(2,1)}, bf16[512,512]{1,0:T(8,128)(2,1)}, u32[]{:S(2)}, u32[]{:S(2)}) collective-permute-start(bf16[512,512]{1,0:T(8,128)(2,1)} %get-tuple-element.64.refs_0_.own_ref), channel_id=1, source_target_pairs={{0,2},{1,3},{2,0},{3,1},{4,6},{5,7},{6,4},{7,5},{8,10},{9,11},{10,... | collective-permute-start | bytes 1572872 | tf_op jit(solution)/shard_map/ppermute | solution.py:546
  28.8 60.0 %collective-permute-start.12 = (bf16[512,512]{1,0:T(8,128)(2,1)}, bf16[512,512]{1,0:T(8,128)(2,1)}, u32[]{:S(2)}, u32[]{:S(2)}) collective-permute-start(bf16[512,512]{1,0:T(8,128)(2,1)} %get-tuple-element.67.refs_0_.own_ref.refs_1_), channel_id=1, source_target_pairs={{0,1},{1,0},{2,3},{3,2},{4,5},{5,4},{6,7},{7,6},{8,9},{9,8},{10,11... | collective-permute-start | bytes 1572872 | tf_op jit(solution)/shard_map/ppermute | solution.py:546
  29.0 27.4 %collective-permute-start.13 = (bf16[512,512]{1,0:T(8,128)(2,1)}, bf16[512,512]{1,0:T(8,128)(2,1)}, u32[]{:S(2)}, u32[]{:S(2)}) collective-permute-start(bf16[512,512]{1,0:T(8,128)(2,1)} %get-tuple-element.67.refs_0_.own_ref.refs_1_), channel_id=1, source_target_pairs={{0,2},{1,3},{2,0},{3,1},{4,6},{5,7},{6,4},{7,5},{8,10},{9,11},{10,... | collective-permute-start | bytes 1572872 | tf_op jit(solution)/shard_map/ppermute | solution.py:546
  29.3 68.3 %collective-permute-start.9 = (bf16[1024,128]{1,0:T(8,128)(2,1)S(1)}, bf16[1024,128]{1,0:T(8,128)(2,1)S(1)}, u32[]{:S(2)}, u32[]{:S(2)}) collective-permute-start(bf16[1024,128]{1,0:T(8,128)(2,1)S(1)} %copy-done.5), channel_id=1, source_target_pairs={{0,2},{1,3},{2,0},{3,1},{4,6},{5,7},{6,4},{7,5},{8,10},{9,11},{10,... | collective-permute-start | bytes 786440 | tf_op jit(solution)/shard_map/ppermute | solution.py:546
  56.5 34.1 %collective-permute-start.14 = (bf16[512,512]{1,0:T(8,128)(2,1)}, bf16[512,512]{1,0:T(8,128)(2,1)}, u32[]{:S(2)}, u32[]{:S(2)}) collective-permute-start(bf16[512,512]{1,0:T(8,128)(2,1)} %collective-permute-done.13.refs_2_), channel_id=1, source_target_pairs={{0,1},{1,0},{2,3},{3,2},{4,5},{5,4},{6,7},{7,6},{8,9},{9,8},{10,11... | collective-permute-start | bytes 1572872 | tf_op jit(solution)/shard_map/ppermute | solution.py:546
  57.6 42.3 %collective-permute-start.7 = (bf16[1024,128]{1,0:T(8,128)(2,1)S(1)}, bf16[1024,128]{1,0:T(8,128)(2,1)S(1)}, u32[]{:S(2)}, u32[]{:S(2)}) collective-permute-start(bf16[1024,128]{1,0:T(8,128)(2,1)S(1)} %copy-done.5), channel_id=1, source_target_pairs={{0,1},{1,0},{2,3},{3,2},{4,5},{5,4},{6,7},{7,6},{8,9},{9,8},{10,11... | collective-permute-start | bytes 786440 | tf_op jit(solution)/shard_map/ppermute | solution.py:546
  64.2 36.2 %collective-permute-start.4 = (bf16[512,512]{1,0:T(8,128)(2,1)}, bf16[512,512]{1,0:T(8,128)(2,1)}, u32[]{:S(2)}, u32[]{:S(2)}) collective-permute-start(bf16[512,512]{1,0:T(8,128)(2,1)} %get-tuple-element.65.refs_0_), channel_id=1, source_target_pairs={{0,2},{1,3},{2,0},{3,1},{4,6},{5,7},{6,4},{7,5},{8,10},{9,11},{10,... | collective-permute-start | bytes 1572872 | tf_op jit(solution)/shard_map/ppermute | solution.py:546
  102.7 23.1 %collective-permute-start.15 = (bf16[512,512]{1,0:T(8,128)(2,1)}, bf16[512,512]{1,0:T(8,128)(2,1)}, u32[]{:S(2)}, u32[]{:S(2)}) collective-permute-start(bf16[512,512]{1,0:T(8,128)(2,1)} %get-tuple-element.68.refs_0_.refs_1_), channel_id=1, source_target_pairs={{0,1},{1,0},{2,3},{3,2},{4,5},{5,4},{6,7},{7,6},{8,9},{9,8},{10,11... | collective-permute-start | bytes 1572872 | tf_op jit(solution)/shard_map/ppermute | solution.py:546
  136.0 60.5 %collective-permute-start.19 = (bf16[1024,128]{1,0:T(8,128)(2,1)}, bf16[1024,128]{1,0:T(8,128)(2,1)}, u32[]{:S(2)}, u32[]{:S(2)}) collective-permute-start(bf16[1024,128]{1,0:T(8,128)(2,1)} %convolution_convert_fusion), channel_id=1, source_target_pairs={{0,1},{1,0},{2,3},{3,2},{4,5},{5,4},{6,7},{7,6},{8,9},{9,8},{10,11... | collective-permute-start | bytes 786440 | tf_op jit(solution)/shard_map/ppermute | solution.py:546
  137.6 67.9 %collective-permute-start.18 = (bf16[1024,128]{1,0:T(8,128)(2,1)}, bf16[1024,128]{1,0:T(8,128)(2,1)}, u32[]{:S(2)}, u32[]{:S(2)}) collective-permute-start(bf16[1024,128]{1,0:T(8,128)(2,1)} %convolution_convert_fusion.1), channel_id=1, source_target_pairs={{0,1},{1,0},{2,3},{3,2},{4,5},{5,4},{6,7},{7,6},{8,9},{9,8},{10,11... | collective-permute-start | bytes 786440 | tf_op jit(solution)/shard_map/ppermute | solution.py:546
  169.8 18.4 %collective-permute-start.60 = (bf16[512,128]{1,0:T(8,128)(2,1)S(1)}, bf16[512,128]{1,0:T(8,128)(2,1)S(1)}, u32[]{:S(2)}, u32[]{:S(2)}) collective-permute-start(bf16[512,128]{1,0:T(8,128)(2,1)S(1)} %convolution_convert_fusion.4), channel_id=1, source_target_pairs={{0,1},{1,0},{2,3},{3,2},{4,5},{5,4},{6,7},{7,6},{8,9},{9,8},{10,11... | collective-permute-start | bytes 393224 | tf_op jit(solution)/shard_map/ppermute | solution.py:546
  190.1 25.8 %collective-permute-start.22 = (bf16[512,1024]{1,0:T(8,128)(2,1)S(1)}, bf16[512,1024]{1,0:T(8,128)(2,1)S(1)}, u32[]{:S(2)}, u32[]{:S(2)}) collective-permute-start(bf16[512,1024]{1,0:T(8,128)(2,1)S(1)} %pad_maximum_fusion.1), channel_id=1, source_target_pairs={{0,1},{1,0},{2,3},{3,2},{4,5},{5,4},{6,7},{7,6},{8,9},{9,8},{10,11... | collective-permute-start | bytes 3145736 | tf_op jit(solution)/shard_map/ppermute | solution.py:546
  202.4 22.1 %collective-permute-start.21 = (bf16[512,1024]{1,0:T(8,128)(2,1)S(1)}, bf16[512,1024]{1,0:T(8,128)(2,1)S(1)}, u32[]{:S(2)}, u32[]{:S(2)}) collective-permute-start(bf16[512,1024]{1,0:T(8,128)(2,1)S(1)} %pad_maximum_fusion), channel_id=1, source_target_pairs={{0,1},{1,0},{2,3},{3,2},{4,5},{5,4},{6,7},{7,6},{8,9},{9,8},{10,11... | collective-permute-start | bytes 3145736 | tf_op jit(solution)/shard_map/ppermute | solution.py:546
  217.3 25.4 %collective-permute-start.23 = (bf16[512,1024]{1,0:T(8,128)(2,1)}, bf16[512,1024]{1,0:T(8,128)(2,1)S(1)}, u32[]{:S(2)}, u32[]{:S(2)}) collective-permute-start(bf16[512,1024]{1,0:T(8,128)(2,1)} %fusion), channel_id=1, source_target_pairs={{0,2},{1,3},{2,0},{3,1},{4,6},{5,7},{6,4},{7,5},{8,10},{9,11},{10,... | collective-permute-start | bytes 3145736 | tf_op jit(solution)/shard_map/ppermute | solution.py:546
  232.3 56.4 %collective-permute-start.46 = (bf16[128,1024]{1,0:T(8,128)(2,1)}, bf16[128,1024]{1,0:T(8,128)(2,1)}, u32[]{:S(2)}, u32[]{:S(2)}) collective-permute-start(bf16[128,1024]{1,0:T(8,128)(2,1)} %get-tuple-element.132), channel_id=1, source_target_pairs={{0,8},{8,16},{16,24},{24,28},{28,20},{20,12},{12,4},{4,0},{1,9},{9... | collective-permute-start | bytes 786440 | tf_op jit(solution)/shard_map/ppermute | solution.py:606
  233.8 57.8 %collective-permute-start.47 = (bf16[128,1024]{1,0:T(8,128)(2,1)S(1)}, bf16[128,1024]{1,0:T(8,128)(2,1)}, u32[]{:S(2)}, u32[]{:S(2)}) collective-permute-start(bf16[128,1024]{1,0:T(8,128)(2,1)S(1)} %get-tuple-element.131), channel_id=1, source_target_pairs={{8,0},{16,8},{24,16},{28,24},{20,28},{12,20},{4,12},{0,4},{9,1},{1... | collective-permute-start | bytes 786440 | tf_op jit(solution)/shard_map/ppermute | solution.py:606
  285.0 56.6 %collective-permute-start.24 = (bf16[512,1024]{1,0:T(8,128)(2,1)}, bf16[512,1024]{1,0:T(8,128)(2,1)S(1)}, u32[]{:S(2)}, u32[]{:S(2)}) collective-permute-start(bf16[512,1024]{1,0:T(8,128)(2,1)} %pad_maximum_fusion.2), channel_id=1, source_target_pairs={{0,1},{1,0},{2,3},{3,2},{4,5},{5,4},{6,7},{7,6},{8,9},{9,8},{10,11... | collective-permute-start | bytes 3145736 | tf_op jit(solution)/shard_map/ppermute | solution.py:546
  288.5 44.6 %collective-permute-start.25 = (bf16[512,1024]{1,0:T(8,128)(2,1)}, bf16[512,1024]{1,0:T(8,128)(2,1)}, u32[]{:S(2)}, u32[]{:S(2)}) collective-permute-start(bf16[512,1024]{1,0:T(8,128)(2,1)} %pad_maximum_fusion.3), channel_id=1, source_target_pairs={{0,1},{1,0},{2,3},{3,2},{4,5},{5,4},{6,7},{7,6},{8,9},{9,8},{10,11... | collective-permute-start | bytes 3145736 | tf_op jit(solution)/shard_map/ppermute | solution.py:546
  323.6 113.4 %collective-permute-start.63 = (bf16[128,1152]{1,0:T(8,128)(2,1)S(1)}, bf16[128,1152]{1,0:T(8,128)(2,1)}, u32[]{:S(2)}, u32[]{:S(2)}) collective-permute-start(bf16[128,1152]{1,0:T(8,128)(2,1)S(1)} %copy-done.33), channel_id=1, source_target_pairs={{0,8},{8,16},{16,24},{24,28},{28,20},{20,12},{12,4},{4,0},{1,9},{9... | collective-permute-start | bytes 884744 | tf_op jit(solution)/shard_map/ppermute | solution.py:594
  340.2 19.5 %collective-permute-start.26 = (bf16[512,1024]{1,0:T(8,128)(2,1)}, bf16[512,1024]{1,0:T(8,128)(2,1)}, u32[]{:S(2)}, u32[]{:S(2)}) collective-permute-start(bf16[512,1024]{1,0:T(8,128)(2,1)} %fusion.1), channel_id=1, source_target_pairs={{0,2},{1,3},{2,0},{3,1},{4,6},{5,7},{6,4},{7,5},{8,10},{9,11},{10,... | collective-permute-start | bytes 3145736 | tf_op jit(solution)/shard_map/ppermute | solution.py:546
  345.6 96.3 %collective-permute-start.56 = (bf16[128,1024]{1,0:T(8,128)(2,1)}, bf16[128,1024]{1,0:T(8,128)(2,1)}, u32[]{:S(2)}, u32[]{:S(2)}) collective-permute-start(bf16[128,1024]{1,0:T(8,128)(2,1)} %collective-permute-done.54), channel_id=1, source_target_pairs={{0,8},{8,16},{16,24},{24,28},{28,20},{20,12},{12,4},{4,0},{1,9},{9... | collective-permute-start | bytes 786440 | tf_op jit(solution)/shard_map/ppermute | solution.py:606
  350.4 86.6 %collective-permute-start.76 = (bf16[128,1152]{1,0:T(8,128)(2,1)S(1)}, bf16[128,1152]{1,0:T(8,128)(2,1)S(1)}, u32[]{:S(2)}, u32[]{:S(2)}) collective-permute-start(bf16[128,1152]{1,0:T(8,128)(2,1)S(1)} %add_convert_fusion.2), channel_id=1, source_target_pairs={{8,0},{16,8},{24,16},{28,24},{20,28},{12,20},{4,12},{0,4},{9,1},{1... | collective-permute-start | bytes 884744 | tf_op jit(solution)/shard_map/ppermute | solution.py:594
  456.0 17.7 %collective-permute-start.80 = (bf16[128,1152]{1,0:T(8,128)(2,1)S(1)}, bf16[128,1152]{1,0:T(8,128)(2,1)S(1)}, u32[]{:S(2)}, u32[]{:S(2)}) collective-permute-start(bf16[128,1152]{1,0:T(8,128)(2,1)S(1)} %collective-permute-done.78), channel_id=1, source_target_pairs={{8,0},{16,8},{24,16},{28,24},{20,28},{12,20},{4,12},{0,4},{9,1},{1... | collective-permute-start | bytes 884744 | tf_op jit(solution)/shard_map/ppermute | solution.py:606
  (112 other events, 1188.7 us)
